TPU v7x, 32 devices: a whole 2x2x4 slice. The times are simulated.
32 devices in a mesh: dp: 8 (over z, core), mp: 4 (over y, x).
Axes of the slice: x: 2, y: 2, z: 4, core: 2. Of those that a mesh axis runs over, the one named last changes fastest.
Arguments:
- layer_in: bfloat16 [1024, 4608], P('dp', 'mp'), may hold values from -6 to 6
- up_grad: bfloat16 [1024, 36864], P('dp', 'mp'), may hold values from -12 to 12
- hidden: bfloat16 [1024, 36864], P('dp', 'mp'), may hold values from -6 to 6
- out_grad: bfloat16 [1024, 4608], P('dp', 'mp'), may hold values from -12 to 12
- err_up_left: bfloat16 [8, 4608, 32], P('dp', 'mp'), may hold values from -12 to 12
- err_up_right: bfloat16 [8, 36864, 32], P('dp', 'mp'), may hold values from -12 to 12
- err_down_left: bfloat16 [8, 36864, 32], P('dp', 'mp'), may hold values from -12 to 12
- err_down_right: bfloat16 [8, 4608, 32], P('dp', 'mp'), may hold values from -12 to 12
- q_up: float32 [36864, 32], P('mp'), may hold values from -6 to 6
- q_down: float32 [4608, 32], P('mp'), may hold values from -6 to 6
- momentum_up: bfloat16 [4608, 36864], P('dp', 'mp'), may hold values from -4 to 4
- momentum_down: bfloat16 [36864, 4608], P('mp', 'dp'), may hold values from -4 to 4
Outputs:
- q_up_next: float32 [36864, 32], P('mp')
- q_down_next: float32 [4608, 32], P('mp')
- new_momentum_up: bfloat16 [4608, 36864], P('dp', 'mp')
- new_momentum_down: bfloat16 [36864, 4608], P('mp', 'dp')
All inputs are finite; a program needn't handle non-finite values.
Results may differ from a plain program's by a relative error of at most 0.001.
Values sent between devices are 32-bit elements; how exact they have to be, the bound alone decides.
A program may use at most 128 MiB of HBM per device.

v0:
```python
import jax
import jax.numpy as jnp
from jax import lax
from jax.sharding import PartitionSpec as P


def times(left, right):
    return jnp.dot(left, right, precision=lax.Precision.HIGHEST, preferred_element_type=jnp.float32)


def solve_factor(factor, gram):
    lower = jnp.linalg.cholesky(gram)
    return jax.scipy.linalg.solve_triangular(lower, factor.T, lower=True).T


def on_device(
    layer_in,
    up_grad,
    hidden,
    out_grad,
    err_up_left,
    err_up_right,
    err_down_left,
    err_down_right,
    q_up,
    q_down,
    momentum_up,
    momentum_down,
):
    replicas = lax.axis_size("dp")
    up_left = err_up_left[0]
    up_right = err_up_right[0]
    down_left = err_down_left[0]
    down_right = err_down_right[0]
    s_up, e_up, s_down, e_down = lax.psum(
        (
            times(up_grad, q_up),
            times(up_right.T, q_up),
            times(out_grad, q_down),
            times(down_right.T, q_down),
        ),
        "mp",
    )
    p_up_rows = times(layer_in.T, s_up) + times(up_left, e_up)
    p_down_rows = times(hidden.T, s_down) + times(down_left, e_down)
    p_up_rows, p_down_rows = lax.psum((p_up_rows, p_down_rows), "dp")
    p_up_rows = p_up_rows / replicas
    p_down_rows = p_down_rows / replicas
    gram_up, gram_down = lax.psum(
        (times(p_up_rows.T, p_up_rows), times(p_down_rows.T, p_down_rows)), "mp"
    )
    orth_up = solve_factor(p_up_rows, gram_up)
    orth_down = solve_factor(p_down_rows, gram_down)
    t_up, f_up, t_down, f_down = lax.psum(
        (
            times(layer_in, orth_up),
            times(up_left.T, orth_up),
            times(hidden, orth_down),
            times(down_left.T, orth_down),
        ),
        "mp",
    )
    q_up_rows = times(up_grad.T, t_up) + times(up_right, f_up)
    q_down_rows = times(out_grad.T, t_down) + times(down_right, f_down)
    q_up_rows, q_down_rows = lax.psum((q_up_rows, q_down_rows), "dp")
    q_up_next = q_up_rows / replicas
    q_down_next = q_down_rows / replicas
    stacked = jnp.stack([orth_up, q_down_next])
    block = momentum_up.shape[0]
    replica = lax.axis_index("dp")
    whole_rows = lax.all_gather(stacked, "mp", axis=1, tiled=True)
    picked = lax.dynamic_slice_in_dim(whole_rows, replica * block, block, 1)
    new_momentum_up = (
        0.9 * momentum_up.astype(jnp.float32) + times(picked[0], q_up_next.T)
    ).astype(jnp.bfloat16)
    new_momentum_down = (
        0.9 * momentum_down.astype(jnp.float32) + times(orth_down, picked[1].T)
    ).astype(jnp.bfloat16)
    return (q_up_next, q_down_next, new_momentum_up, new_momentum_down)


def solution(mesh):
    return jax.shard_map(
        on_device,
        mesh=mesh,
        in_specs=(
            P("dp", "mp"),
            P("dp", "mp"),
            P("dp", "mp"),
            P("dp", "mp"),
            P("dp", "mp", None),
            P("dp", "mp", None),
            P("dp", "mp", None),
            P("dp", "mp", None),
            P("mp", None),
            P("mp", None),
            P("dp", "mp"),
            P("mp", "dp"),
        ),
        out_specs=(P("mp", None), P("mp", None), P("dp", "mp"), P("mp", "dp")),
        check_vma=False,
    )
```

profile of v0, /device:TPU:0, one launch (start us, length us, event | category | flops | bytes accessed | tf_op | source)
XLA Modules:
  0.0 305.4 jit_solution(5136944613755599154)
XLA Ops:
  7.2 0.0 all-reduce.10.cloned.1.call-start
  7.2 2.3 fusion.13
  9.6 4.3 %fusion.40 = f32[128,32]{1,0:T(8,128)} fusion(bf16[128,9216]{1,0:T(8,128)(2,1)} %param.14, f32[9216,32]{0,1:T(8,128)S(1)} %copy-done.3), kind=kOutput, calls=%fused_computation.65 | convolution fusion | flops 452984832 | bytes 3555328 | tf_op jit(solution)/shard_map/dot_general | solution.py:8
  14.0 0.2 fusion.22
  14.2 0.4 fusion.42
  14.6 20.5 %all-reduce.4 = (f32[128,32]{1,0:T(8,128)S(1)}, f32[32,32]{1,0:T(8,128)S(1)}, f32[32,32]{1,0:T(8,128)S(1)}, f32[128,32]{1,0:T(8,128)S(1)}) all-reduce(f32[128,32]{1,0:T(8,128)} %fusion.40, f32[32,32]{1,0:T(8,128)S(1)} %fusion.13, f32[32,32]{1,0:T(8,128)S(1)} %fusion.22, f32[128,32]{1,0:T(8,128)S(1)} %fusion.42), channel_id=1, replica_groups=mesh['dp'=8,'mp'=4] {'mp'}, use_global_device_ids=true, to_apply=%region_0.0 | all-reduce | flops 10240 | bytes 81920 | tf_op jit(solution)/shard_map/psum | solution.py:35
  35.1 1.3 fusion.41
  36.4 0.7 fusion.9
  37.1 0.9 fusion.2
  38.0 2.1 fusion
  40.2 0.0 all-reduce.10.cloned.1.call-update
  40.2 0.0 all-reduce.8.cloned.1.call-start
  40.2 59.6 %all-reduce.10.cloned.1.call-done = (f32[1152,32]{0,1:T(8,128)}, f32[9216,32]{0,1:T(8,128)}) async-done(((f32[1152,32]{0,1:T(8,128)}, f32[9216,32]{0,1:T(8,128)}), (f32[1152,32]{0,1:T(8,128)}, f32[9216,32]{0,1:T(8,128)})) %all-reduce.10.cloned.1.call-update) | async-done | bytes 1327120 | tf_op jit(solution)/shard_map/psum | solution.py:46
  99.9 1.3 fusion.19
  101.2 2.9 fusion.6
  104.1 16.5 %all-reduce.3 = (f32[32,32]{0,1:T(8,128)S(1)}, f32[32,32]{0,1:T(8,128)S(1)}) all-reduce(f32[32,32]{0,1:T(8,128)S(1)} %fusion.19, f32[32,32]{0,1:T(8,128)S(1)} %fusion.6), channel_id=1, replica_groups=mesh['dp'=8,'mp'=4] {'mp'}, use_global_device_ids=true, to_apply=%region_3.0 | all-reduce | flops 2048 | bytes 16384 | tf_op jit(solution)/shard_map/psum | solution.py:49
  120.5 0.1 copy.17
  120.6 0.1 copy.19
  120.7 2.9 cholesky.44
  123.7 0.6 compare_reduce_fusion.1
  124.3 0.7 fusion.28
  125.0 2.4 custom-call.10
  127.4 0.4 fusion.17
  127.8 0.8 convolution_bitcast_fusion.2
  128.6 1.0 convolution_bitcast_fusion.3
  129.6 2.9 cholesky.55
  132.6 0.6 compare_reduce_fusion
  133.2 0.7 fusion.29
  133.9 2.4 custom-call.11
  136.3 2.5 fusion.4
  138.8 0.7 convolution_bitcast_fusion.1
  139.5 2.9 convolution_bitcast_fusion
  142.4 15.8 %all-reduce.2 = (f32[32,32]{0,1:T(8,128)}, f32[128,32]{0,1:T(8,128)}, f32[128,32]{0,1:T(8,128)}, f32[32,32]{0,1:T(8,128)}) all-reduce(f32[32,32]{0,1:T(8,128)} %convolution_bitcast_fusion.2, f32[128,32]{0,1:T(8,128)} %convolution_bitcast_fusion.3, f32[128,32]{0,1:T(8,128)} %convolution_bitcast_fusion, ...), channel_id=1, replica_groups=mesh['dp'=8,'mp'=4] {'mp'}, use_global_device_ids=true, to_apply=%region_7.9 | all-reduce | flops 10240 | bytes 81920 | tf_op jit(solution)/shard_map/psum | solution.py:54
  158.2 1.4 fusion.43
  159.6 1.7 fusion.11
  161.3 0.9 fusion.3
  162.2 2.1 fusion.1
  164.2 0.0 all-reduce.8.cloned.1.call-update
  164.2 0.3 all-gather.2.cloned.1.call-start
  164.5 59.1 %all-reduce.8.cloned.1.call-done = (f32[9216,32]{0,1:T(8,128)}, f32[1152,32]{0,1:T(8,128)}) async-done(((f32[9216,32]{0,1:T(8,128)}, f32[1152,32]{0,1:T(8,128)}), (f32[9216,32]{0,1:T(8,128)}, f32[1152,32]{0,1:T(8,128)})) %all-reduce.8.cloned.1.call-update) | async-done | bytes 1327120 | tf_op jit(solution)/shard_map/psum | solution.py:65
  223.6 0.9 fusion.70
  224.5 1.6 broadcast_multiply_fusion.1
  226.1 1.7 pad_maximum_fusion
  227.8 0.0 all-gather.2.cloned.1.call-update
  227.8 2.4 broadcast_multiply_fusion
  230.1 25.5 %all-gather.2.cloned.1.call-done = f32[2,4608,32]{1,2,0:T(8,128)} async-done(((f32[2,1152,32]{1,2,0:T(8,128)}), f32[2,4608,32]{1,2,0:T(8,128)}) %all-gather.2.cloned.1.call-update) | async-done | bytes 1179664 | tf_op jit(solution)/shard_map/all_gather | solution.py:71
  255.6 21.7 %add_convert_fusion = bf16[9216,576]{0,1:T(8,128)(2,1)} fusion(bf16[9216,576]{0,1:T(8,128)(2,1)} %param.24, f32[32,9216]{1,0:T(8,128)S(1)} %fusion.4, f32[2,4608,32]{1,2,0:T(8,128)} %all-gather.2.cloned.1.call-done, s32[]{:T(128)S(6)} %add.89, s32[]{:T(128)S(6)} %select_n.6), kind=kOutput, calls=%fused_computation | convolution fusion | flops 2059665408 | bytes 22495240 | tf_op jit(solution)/shard_map/dot_general | solution.py:8
  277.3 21.6 %add_convert_fusion.1 = bf16[576,9216]{1,0:T(8,128)(2,1)} fusion(bf16[576,9216]{1,0:T(8,128)(2,1)} %param.23, f32[9216,32]{0,1:T(8,128)S(1)} %copy-done.2, f32[2,4608,32]{1,2,0:T(8,128)} %all-gather.2.cloned.1.call-done, s32[]{:T(128)S(6)} %select_n.6), kind=kOutput, calls=%fused_computation.1 | convolution fusion | flops 2059665408 | bytes 22495236 | tf_op jit(solution)/shard_map/dot_general | solution.py:8
  (35 shorter events, 0.2 us)
Async XLA Ops:
  7.2 30.9 %copy-start = (bf16[128,9216]{1,0:T(8,128)(2,1)S(1)}, bf16[128,9216]{1,0:T(8,128)(2,1)}, u32[]{:S(2)}) copy-start(bf16[128,9216]{1,0:T(8,128)(2,1)} %param.15) | copy-start | bytes 7077892
  7.2 2.4 copy-start.3
  7.2 92.7 %all-reduce.10.cloned.1.call-start = ((), (), s32[]{:S(2)}) async-start(), calls=%async_computation.2 | async-start | bytes 2654208 | tf_op jit(solution)/shard_map/psum | solution.py:46
  9.6 4.4 %copy-start.10 = (f32[1152,32]{0,1:T(8,128)S(1)}, f32[1152,32]{0,1:T(8,128)}, u32[]{:S(2)}) copy-start(f32[1152,32]{0,1:T(8,128)} %param.22) | copy-start | bytes 442372
  9.6 4.4 %copy-start.12 = (bf16[1,1152,32]{1,2,0:T(8,128)(2,1)S(1)}, bf16[1,1152,32]{1,2,0:T(8,128)(2,1)}, u32[]{:S(2)}) copy-start(bf16[1,1152,32]{1,2,0:T(8,128)(2,1)} %param.20) | copy-start | bytes 221188
  9.6 4.6 %copy-start.8 = (bf16[128,1152]{1,0:T(8,128)(2,1)S(1)}, bf16[128,1152]{1,0:T(8,128)(2,1)}, u32[]{:S(2)}) copy-start(bf16[128,1152]{1,0:T(8,128)(2,1)} %param.16) | copy-start | bytes 884740
  14.0 22.5 %copy-start.4 = (bf16[1,9216,32]{1,2,0:T(8,128)(2,1)S(1)}, bf16[1,9216,32]{1,2,0:T(8,128)(2,1)}, u32[]{:S(2)}) copy-start(bf16[1,9216,32]{1,2,0:T(8,128)(2,1)} %param.19) | copy-start | bytes 1769476
  35.1 2.0 copy-start.11
  40.2 88.4 %copy-start.7 = (bf16[128,1152]{1,0:T(8,128)(2,1)S(1)}, bf16[128,1152]{1,0:T(8,128)(2,1)}, u32[]{:S(2)}) copy-start(bf16[128,1152]{1,0:T(8,128)(2,1)} %param.13) | copy-start | bytes 884740
  40.2 183.4 %all-reduce.8.cloned.1.call-start = ((), (), s32[]{:S(2)}) async-start(), calls=%async_computation.1 | async-start | bytes 2654208 | tf_op jit(solution)/shard_map/psum | solution.py:65
  99.9 27.5 %copy-start.9 = (f32[1152,32]{0,1:T(8,128)S(1)}, f32[1152,32]{0,1:T(8,128)}, u32[]{:S(2)}) copy-start(f32[1152,32]{0,1:T(8,128)} %get-tuple-element.7) | copy-start | bytes 442372
  127.8 0.8 copy-start.6
  136.3 2.5 copy-start.5
  158.2 3.1 %copy-start.13 = (bf16[1,1152,32]{1,2,0:T(8,128)(2,1)S(1)}, bf16[1,1152,32]{1,2,0:T(8,128)(2,1)}, u32[]{:S(2)}) copy-start(bf16[1,1152,32]{1,2,0:T(8,128)(2,1)} %param.20) | copy-start | bytes 221188
  158.2 3.1 %copy-start.15 = (f32[32,32]{0,1:T(8,128)S(1)}, f32[32,32]{0,1:T(8,128)}, u32[]{:S(2)}) copy-start(f32[32,32]{0,1:T(8,128)} %get-tuple-element.12) | copy-start | bytes 12292
  158.2 4.0 %copy-start.1 = (bf16[128,9216]{1,0:T(8,128)(2,1)S(1)}, bf16[128,9216]{1,0:T(8,128)(2,1)}, u32[]{:S(2)}) copy-start(bf16[128,9216]{1,0:T(8,128)(2,1)} %param.14) | copy-start | bytes 7077892
  159.6 2.6 copy-start.14
  164.2 91.4 %all-gather.2.cloned.1.call-start = ((), (), s32[]{:S(2)}) async-start(), calls=%async_computation | async-start | bytes 1474560 | tf_op jit(solution)/shard_map/all_gather | solution.py:71
  255.6 21.7 %copy-start.2 = (f32[9216,32]{0,1:T(8,128)S(1)}, f32[9216,32]{0,1:T(8,128)}, u32[]{:S(2)}) copy-start(f32[9216,32]{0,1:T(8,128)} %broadcast_multiply_fusion) | copy-start | bytes 3538948
Sparse Core Ops, SparseCore 0:
  40.3 59.5 all-reduce.9
  164.4 59.1 all-reduce.7
  227.9 27.6 all-gather.1
where the time goes:
time: 306 us; the launch traced here: 305 us
  waiting for transfers between devices  144 us (47%)
  matrix products  73.9 us (24%)
  blocking collectives  52.7 us (17%)
  other arithmetic  19.9 us (7%)
  between operations  14 us (5%)
    dot_general x20, matrix products, times(): jnp.dot(left, right, precision=lax.Precision.HIGHEST, preferred_element_t...  71.1 us
    psum x1, waiting for transfers between devices, on_device(): p_up_rows, p_down_rows = lax.psum((p_up_rows, p_down_rows), 'dp')  59.6 us
    psum x1, waiting for transfers between devices, on_device(): q_up_rows, q_down_rows = lax.psum((q_up_rows, q_down_rows), 'dp')  59.1 us
    all_gather x1, waiting for transfers between devices, on_device(): whole_rows = lax.all_gather(stacked, 'mp', axis=1, tiled=True)  25.5 us
    psum x1, blocking collectives, on_device(): lax.psum((times(up_grad, q_up), times(up_right.T, q_up), times(out_grad,...  20.5 us
    psum x1, blocking collectives, on_device(): lax.psum((times(p_up_rows.T, p_up_rows), times(p_down_rows.T, p_down_rows...  16.5 us
    psum x1, blocking collectives, on_device(): lax.psum((times(layer_in, orth_up), times(up_left.T, orth_up), times(hidd...  15.8 us
    another operation x6, other arithmetic, solve_factor(): lower = jnp.linalg.cholesky(gram)  7.18 us
  transfers between devices with their start and end apart: 3, of which 3 were waited for; matrix products, arithmetic and copies ran while one was open for 1% of the time, Pallas kernels for 0%

commit v1 on v0

v1 whole, which is shorter than its diff:
```python
import functools

import jax
import jax.numpy as jnp
from jax import lax
from jax.experimental import pallas as pl
from jax.experimental.pallas import tpu as pltpu
from jax.sharding import PartitionSpec as P

F32 = jnp.float32
BF16 = jnp.bfloat16
MESH = pl.DeviceIdType.MESH
LANES = 128
MAX_CHUNK = 1152


def whole_tiles(width):
    return -(-width // LANES) * LANES


def chunk_of(width):
    if width % LANES:
        return width
    size = MAX_CHUNK
    while width % size:
        size -= LANES
    return size


def split3(x):
    hi = x.astype(BF16)
    rest = x - hi.astype(F32)
    mid = rest.astype(BF16)
    lo = (rest - mid.astype(F32)).astype(BF16)
    return jnp.concatenate([hi, mid, lo], axis=0)


def fold3(x):
    rank = x.shape[0] // 3
    return x[:rank] + x[rank : 2 * rank] + x[2 * rank :]


def dot_nt(a, b):
    return lax.dot_general(a, b, (((1,), (1,)), ((), ())), preferred_element_type=F32)


def dot_nn(a, b):
    return jnp.dot(a, b, preferred_element_type=F32)


def dot_small(a, b):
    return jnp.dot(a, b, precision=lax.Precision.HIGHEST, preferred_element_type=F32)


def project(x_ref, start, rows_ref, err_ref, with_gram):
    width = rows_ref.shape[1]
    step = chunk_of(width)
    outs = rows_ref.shape[0] + err_ref.shape[0] + (3 * err_ref.shape[0] if with_gram else 0)

    def body(i, acc):
        at = 0 if step == width else pl.multiple_of(i * step, LANES)
        x = split3(x_ref[:, pl.ds(start + at, step)])
        parts = [rows_ref[:, pl.ds(at, step)], err_ref[:, pl.ds(at, step)]]
        if with_gram:
            parts.append(x)
        return acc + dot_nt(x, jnp.concatenate(parts, axis=0))

    zero = jnp.zeros((3 * err_ref.shape[0], outs), F32)
    return body(0, zero) if step == width else lax.fori_loop(0, width // step, body, zero)


def expand(left, rows_ref, err_ref, out_ref, start):
    width = rows_ref.shape[1]
    step = chunk_of(width)
    stacked = split3(left)

    def body(i, carry):
        at = 0 if step == width else pl.multiple_of(i * step, LANES)
        right = jnp.concatenate([rows_ref[:, pl.ds(at, step)], err_ref[:, pl.ds(at, step)]], axis=0)
        out_ref[:, pl.ds(start + at, step)] = fold3(dot_nn(stacked, right))
        return carry

    if step == width:
        body(0, 0)
    else:
        lax.fori_loop(0, width // step, body, 0)


def gram_and_projections(acc, tokens):
    rank = acc.shape[0] // 3
    high, middle = acc[:rank], acc[rank : 2 * rank]
    low = acc[2 * rank :]
    total = high + middle + low
    tail = total[:, tokens:]
    both = (high + middle)[:, tokens:]
    first = high[:, tokens:]
    lane = lax.broadcasted_iota(jnp.int32, tail.shape, 1)
    gram = tail + pltpu.roll(both, 3 * rank, 1) + pltpu.roll(first, 2 * rank, 1)
    return total[:, :tokens], jnp.where(lane < rank, tail, gram)


def inverse_factors(gram_up, gram_down):
    rank = gram_up.shape[0]
    shape = (rank, 4 * rank)
    lane = lax.broadcasted_iota(jnp.int32, shape, 1)
    row = lax.broadcasted_iota(jnp.int32, shape, 0)
    part = lane // rank
    eye = ((lane - part * rank) == row).astype(F32)
    grams = jnp.where(part == 0, pltpu.roll(gram_up, 3 * rank, 1), pltpu.roll(gram_down, rank, 1))
    a = jnp.where((part == 0) | (part == 2), grams, eye)
    low = lane < 2 * rank
    for k in range(rank - 1):
        pivot_row = a[k : k + 1, :]
        column = jnp.where(low, a[:, k : k + 1], a[:, 2 * rank + k : 2 * rank + k + 1])
        pivot = jnp.where(
            low[:1], pivot_row[:, k : k + 1], pivot_row[:, 2 * rank + k : 2 * rank + k + 1]
        )
        scaled = pivot_row / pivot
        a = a - jnp.where(row > k, column, 0.0) * scaled
    diag_up = jnp.sum(jnp.where(lane == row, a, 0.0), axis=1, keepdims=True)
    diag_down = jnp.sum(jnp.where(lane == row + 2 * rank, a, 0.0), axis=1, keepdims=True)
    a = a / jnp.sqrt(jnp.where(low, diag_up, diag_down))
    return pltpu.roll(a, 3 * rank, 1)[:, :rank], pltpu.roll(a, rank, 1)[:, :rank]


def exchange_kernel(
    n_dp,
    n_mp,
    layer_in,
    up_grad,
    hidden,
    out_grad,
    eul,
    eur,
    edl,
    edr,
    q_up,
    q_down,
    q_up_out,
    q_down_out,
    a_up,
    b_up,
    a_down,
    b_down,
    pay_a,
    got_a,
    pay_b,
    got_b,
    work_p,
    core_p,
    right_p,
    left_p,
    full_p,
    work_q,
    core_q,
    right_q,
    left_q,
    full_q,
    p_block,
    q_block,
    mp_send,
    mp_recv,
    core_sem,
    line_send,
    line_recv,
    pair_send,
    pair_recv,
    block_send,
    block_recv,
):
    dp = lax.axis_index("dp")
    mp = lax.axis_index("mp")
    chips = n_dp // 2
    chip = dp // 2
    core = lax.rem(dp, 2)
    tokens = layer_in.shape[0]
    rank = eul.shape[0]
    small = layer_in.shape[1]
    small_pad = whole_tiles(small)
    large = hidden.shape[1]
    block = a_up.shape[1]
    per_shard = small // block
    owner = dp // per_shard
    half = core_p.shape[1]
    piece = half // (chips // 4)
    mate = (dp + 1 - 2 * core, mp)
    right = (dp + 2, mp)
    left = (dp - 2, mp)

    barrier = pltpu.get_barrier_semaphore()

    def greet(to):
        pl.semaphore_signal(barrier, inc=1, device_id=to, device_id_type=MESH)

    for j in range(1, n_mp):
        greet((dp, lax.rem(mp + j, n_mp)))
    greet(mate)

    @pl.when(chip > 0)
    def _():
        greet(left)

    @pl.when(chip < chips - 1)
    def _():
        greet(right)

    ends = jnp.where(chip > 0, 1, 0) + jnp.where(chip < chips - 1, 1, 0)
    pl.semaphore_wait(barrier, n_mp + ends)

    def remote(src, dst, send, recv, to):
        return pltpu.make_async_remote_copy(
            src_ref=src, dst_ref=dst, send_sem=send, recv_sem=recv, device_id=to, device_id_type=MESH
        )

    def sum_over_mp(pay, got, which):
        copies = []
        for j in range(1, n_mp):
            copies.append(
                remote(
                    pay,
                    got.at[j],
                    mp_send.at[which, j],
                    mp_recv.at[which, j],
                    (dp, lax.rem(mp + j, n_mp)),
                )
            )
            copies[-1].start()
        for c in copies:
            c.wait()
        got[0] = pay[...]
        total = got[lax.rem(mp, n_mp)]
        for i in range(1, n_mp):
            total = total + got[lax.rem(mp + n_mp - i, n_mp)]
        return total

    def all_reduce(work, pair, to_right, to_left, full, which):
        def at_piece(ref, s, base):
            rows = pl.ds(pl.multiple_of(8 * lax.rem(s, 4), 8), 8)
            return ref.at[rows, pl.ds(pl.multiple_of(base + (s // 4) * piece, LANES), piece)]

        mine = core * half
        theirs = (1 - core) * half
        swap = remote(
            work.at[:, pl.ds(pl.multiple_of(theirs, LANES), half)],
            pair,
            core_sem.at[which, 0],
            core_sem.at[which, 1],
            mate,
        )
        swap.start()
        swap.wait()

        own = pl.ds(pl.multiple_of(mine, LANES), half)
        pair[...] += work[:, own]

        def hop(buf, way, s, to):
            return remote(
                at_piece(buf, s, 0),
                at_piece(buf, s, 0),
                line_send.at[which, way, s],
                line_recv.at[which, way, s],
                to,
            )

        def hop_first(buf, way, s, to):
            return remote(
                at_piece(pair, s, 0),
                at_piece(buf, s, 0),
                line_send.at[which, way, s],
                line_recv.at[which, way, s],
                to,
            )

        def add_own(buf, s):
            at = at_piece(buf, s, 0)
            at[...] = at[...] + at_piece(pair, s, 0)[...]

        def reduce_step(k, carry):
            s = chips - 1 - k + chip

            @pl.when((k >= chip) & (chip < chips - 1))
            def _():
                @pl.when(chip > 0)
                def _():
                    hop(to_right, 0, s, right).wait_recv()
                    add_own(to_right, s)
                    hop(to_right, 0, s, right).start()

                @pl.when(chip == 0)
                def _():
                    hop_first(to_right, 0, s, right).start()

            z = k - (chips - 1 - chip)

            @pl.when((z >= 0) & (chip > 0))
            def _():
                @pl.when(chip < chips - 1)
                def _():
                    hop(to_left, 1, z, left).wait_recv()
                    add_own(to_left, z)
                    hop(to_left, 1, z, left).start()

                @pl.when(chip == chips - 1)
                def _():
                    hop_first(to_left, 1, z, left).start()

            return carry

        lax.fori_loop(0, chips - 1, reduce_step, 0)

        mine_here = at_piece(pair, chip, 0)

        @pl.when(chip > 0)
        def _():
            hop(to_right, 0, chip, right).wait_recv()
            mine_here[...] = mine_here[...] + at_piece(to_right, chip, 0)[...]

        @pl.when(chip < chips - 1)
        def _():
            hop(to_left, 1, chip, left).wait_recv()
            mine_here[...] = mine_here[...] + at_piece(to_left, chip, 0)[...]

        at_piece(full, chip, mine)[...] = mine_here[...] * (1.0 / n_dp)

        def spread(way, s, to):
            return remote(
                at_piece(full, s, mine),
                at_piece(full, s, mine),
                line_send.at[which, 2 + way, s],
                line_recv.at[which, 2 + way, s],
                to,
            )

        def to_mate(s):
            return remote(
                at_piece(full, s, mine),
                at_piece(full, s, mine),
                pair_send.at[which, s],
                pair_recv.at[which, s],
                mate,
            )

        def from_mate(s):
            return remote(
                at_piece(full, s, theirs),
                at_piece(full, s, theirs),
                pair_send.at[which, s],
                pair_recv.at[which, s],
                mate,
            )

        def spread_step(t, carry):
            s = chip - t

            @pl.when(s >= 0)
            def _():
                @pl.when(t > 0)
                def _():
                    spread(0, s, right).wait_recv()

                @pl.when(chip < chips - 1)
                def _():
                    spread(0, s, right).start()

            z = chip + t

            @pl.when(z < chips)
            def _():
                @pl.when(t > 0)
                def _():
                    spread(1, z, left).wait_recv()

                @pl.when(chip > 0)
                def _():
                    spread(1, z, left).start()

            @pl.when(s >= 0)
            def _():
                to_mate(s).start()

            @pl.when((z < chips) & (t > 0))
            def _():
                to_mate(z).start()

            return carry

        lax.fori_loop(0, chips, spread_step, 0)

        def drain(s, carry):
            from_mate(s).wait_recv()
            to_mate(s).wait_send()

            @pl.when(chip < s)
            def _():
                hop(to_right, 0, s, right).wait_send()

            @pl.when(chip > s)
            def _():
                hop(to_left, 1, s, left).wait_send()

            @pl.when((s <= chip) & (chip < chips - 1))
            def _():
                spread(0, s, right).wait_send()

            @pl.when((s >= chip) & (chip > 0))
            def _():
                spread(1, s, left).wait_send()

            return carry

        lax.fori_loop(0, chips, drain, 0)

    def send_block(buf, which):
        for j in range(1, n_mp):
            remote(
                buf, buf, block_send.at[which, j], block_recv.at[which], (dp, lax.rem(mp + j, n_mp))
            ).start()

    def wait_block(buf, which):
        @pl.when(mp == owner)
        def _():
            for j in range(1, n_mp):
                remote(
                    buf,
                    buf,
                    block_send.at[which, j],
                    block_recv.at[which],
                    (dp, lax.rem(mp + j, n_mp)),
                ).wait_send()

        @pl.when(mp != owner)
        def _():
            remote(
                buf, buf, block_send.at[which, 1], block_recv.at[which], (dp, lax.rem(mp + 1, n_mp))
            ).wait_recv()

    def pick_block(full, buf):
        shift = lax.rem(small_pad - lax.rem(dp, per_shard) * block, small_pad)
        rolled = pltpu.roll(full[:, :small_pad], shift, 1)
        buf[...] = rolled[:, : buf.shape[1]]

    pay_a[...] = jnp.zeros_like(pay_a)
    pay_a[0, :, : tokens + rank] = fold3(project(q_up, 0, up_grad, eur, False))
    pay_a[1, :, : tokens + rank] = fold3(project(q_down, 0, out_grad, edr, False))
    total = sum_over_mp(pay_a, got_a, 0)

    for work in (work_p, work_q):
        for a, b in ((small // LANES * LANES, small_pad), (small_pad + large, work.shape[1])):
            if b > a:
                work[:, a:b] = jnp.zeros((rank, b - a), F32)
    expand(total[0, :, : tokens + rank], layer_in, eul, work_p, 0)
    expand(total[1, :, : tokens + rank], hidden, edl, work_p, small_pad)
    all_reduce(work_p, core_p, right_p, left_p, full_p, 0)

    @pl.when(mp == owner)
    def _():
        pick_block(full_p, p_block)
        send_block(p_block, 0)

    for i, (start, rows, err) in enumerate(((0, layer_in, eul), (small_pad, hidden, edl))):
        first, second = gram_and_projections(project(full_p, start, rows, err, True), tokens)
        pay_b[i, :, :tokens] = first
        pay_b[i, :, tokens:] = second
    total = sum_over_mp(pay_b, got_b, 1)
    inv_up, inv_down = inverse_factors(total[0, :, tokens:], total[1, :, tokens:])
    t_up = dot_small(inv_up, total[0])[:, : tokens + rank]
    t_down = dot_small(inv_down, total[1])[:, : tokens + rank]
    expand(t_down, out_grad, edr, work_q, 0)
    expand(t_up, up_grad, eur, work_q, small_pad)
    all_reduce(work_q, core_q, right_q, left_q, full_q, 1)

    @pl.when(mp == owner)
    def _():
        pick_block(full_q, q_block)
        send_block(q_block, 1)

    q_down_out[...] = full_q[:, :small]

    def split_left(x):
        hi = x.astype(BF16)
        return jnp.concatenate([hi, hi, (x - hi.astype(F32)).astype(BF16)], axis=0)

    def split_right(x):
        hi = x.astype(BF16)
        return jnp.concatenate([hi, (x - hi.astype(F32)).astype(BF16), hi], axis=0)

    step = chunk_of(large)

    def finish(i, carry):
        at = pl.multiple_of(i * step, LANES)
        orth = dot_small(inv_down, full_p[:, pl.ds(small_pad + at, step)])
        b_down[:, pl.ds(at, step)] = split_right(orth)
        q = full_q[:, pl.ds(small_pad + at, step)]
        q_up_out[:, pl.ds(at, step)] = q
        b_up[:, pl.ds(at, step)] = split_right(q)
        return carry

    lax.fori_loop(0, large // step, finish, 0)

    wait_block(p_block, 0)
    a_up[...] = split_left(dot_small(inv_up, p_block[...]))[:, :block]
    wait_block(q_block, 1)
    a_down[...] = split_left(q_block[...])[:, :block]


def momentum_kernel(m_up, m_down, a_up, b_up, a_down, b_down, out_up, out_down):
    for m, a, b, out in ((m_up, a_up, b_up, out_up), (m_down, a_down, b_down, out_down)):
        delta = lax.dot_general(
            a[...], b[...], (((0,), (0,)), ((), ())), preferred_element_type=F32
        )
        out[...] = (0.9 * m[...].astype(F32) + delta).astype(BF16)


def on_device(
    layer_in,
    up_grad,
    hidden,
    out_grad,
    err_up_left,
    err_up_right,
    err_down_left,
    err_down_right,
    q_up,
    q_down,
    momentum_up,
    momentum_down,
):
    n_dp = lax.axis_size("dp")
    n_mp = lax.axis_size("mp")
    chips = n_dp // 2
    tokens, small = layer_in.shape
    large = hidden.shape[1]
    rank = q_up.shape[1]
    block = momentum_up.shape[0]
    block_pad = whole_tiles(block)
    pieces = n_dp // 4
    piece = -(-((whole_tiles(small) + large) // LANES) // pieces) * LANES
    half = piece * pieces // 2
    vmem = pl.BlockSpec(memory_space=pltpu.VMEM)
    dma = pltpu.SemaphoreType.DMA
    reduce_buffers = [
        pltpu.VMEM((rank, 2 * half), F32),
        pltpu.VMEM((rank, half), F32),
        pltpu.VMEM((rank, half), F32),
        pltpu.VMEM((rank, half), F32),
        pltpu.VMEM((rank, 2 * half), F32),
    ]
    pay = pltpu.VMEM((2, rank, tokens + 4 * rank), F32)
    got = pltpu.VMEM((n_mp, 2, rank, tokens + 4 * rank), F32)
    q_up_t, q_down_t, a_up, b_up, a_down, b_down = pl.pallas_call(
        functools.partial(exchange_kernel, n_dp, n_mp),
        out_shape=(
            jax.ShapeDtypeStruct((rank, large), F32),
            jax.ShapeDtypeStruct((rank, small), F32),
            jax.ShapeDtypeStruct((3 * rank, block), BF16),
            jax.ShapeDtypeStruct((3 * rank, large), BF16),
            jax.ShapeDtypeStruct((3 * rank, block), BF16),
            jax.ShapeDtypeStruct((3 * rank, large), BF16),
        ),
        in_specs=[vmem] * 10,
        out_specs=[vmem] * 6,
        scratch_shapes=[
            pay,
            got,
            pay,
            got,
            *reduce_buffers,
            *reduce_buffers,
            pltpu.VMEM((rank, block_pad), F32),
            pltpu.VMEM((rank, block_pad), F32),
            dma((2, n_mp)),
            dma((2, n_mp)),
            dma((2, 2)),
            dma((2, 4, chips)),
            dma((2, 4, chips)),
            dma((2, chips)),
            dma((2, chips)),
            dma((2, n_mp)),
            dma((2,)),
        ],
        compiler_params=pltpu.CompilerParams(
            collective_id=0, has_side_effects=True, vmem_limit_bytes=30 * 1024 * 1024
        ),
    )(
        layer_in,
        up_grad,
        hidden,
        out_grad,
        err_up_left[0].T,
        err_up_right[0].T,
        err_down_left[0].T,
        err_down_right[0].T,
        q_up.T,
        q_down.T,
    )
    step = chunk_of(large)
    wide = pl.BlockSpec((block, step), lambda i: (0, i))
    left = pl.BlockSpec((3 * rank, block), lambda i: (0, 0))
    right = pl.BlockSpec((3 * rank, step), lambda i: (0, i))
    new_up, new_down_t = pl.pallas_call(
        momentum_kernel,
        grid=(large // step,),
        out_shape=(
            jax.ShapeDtypeStruct((block, large), BF16),
            jax.ShapeDtypeStruct((block, large), BF16),
        ),
        in_specs=[wide, wide, left, right, left, right],
        out_specs=[wide, wide],
        compiler_params=pltpu.CompilerParams(vmem_limit_bytes=32 * 1024 * 1024),
    )(momentum_up, momentum_down.T, a_up, b_up, a_down, b_down)
    return (q_up_t.T, q_down_t.T, new_up, new_down_t.T)


def solution(mesh):
    return jax.shard_map(
        on_device,
        mesh=mesh,
        in_specs=(
            P("dp", "mp"),
            P("dp", "mp"),
            P("dp", "mp"),
            P("dp", "mp"),
            P("dp", "mp", None),
            P("dp", "mp", None),
            P("dp", "mp", None),
            P("dp", "mp", None),
            P("mp", None),
            P("mp", None),
            P("dp", "mp"),
            P("mp", "dp"),
        ),
        out_specs=(P("mp", None), P("mp", None), P("dp", "mp"), P("mp", "dp")),
        check_vma=False,
    )
```

time: 306 us -> 128 us (0.42)
  waiting for transfers between devices: 144 us -> 0 us
  Pallas kernels: 0 us -> 110 us
  matrix products: 73.9 us -> 0 us
  blocking collectives: 52.7 us -> 0 us
  other arithmetic: 19.9 us -> 0 us
  local copies, waits for them, and re-layouts: 0.23 us -> 17 us
  between operations: 14 us -> 0.67 us
    psum x2 -> x0, waiting for transfers between devices: 119 us -> none  [the longest x1 59.6 us: on_device(): p_up_rows, p_down_rows = lax.psum((p_up_rows, p_down_rows), 'dp')]
    pallas_call x0 -> x2, Pallas kernels: none -> 110 us  [the longest x1 95.6 us: on_device(): pl.pallas_call(functools.partial(exchange_kernel, n_dp, n_mp), out_shape=...]
    dot_general x20 -> x0, matrix products: 71.1 us -> none  [times(): jnp.dot(left, right, precision=lax.Precision.HIGHEST, preferred_element_t...]
    psum x3 -> x0, blocking collectives: 52.7 us -> none  [the longest x1 20.5 us: on_device(): lax.psum((times(up_grad, q_up), times(up_right.T, q_up), times(out_grad,...]
    all_gather x1 -> x0, waiting for transfers between devices: 25.5 us -> none  [on_device(): whole_rows = lax.all_gather(stacked, 'mp', axis=1, tiled=True)]
    unnamed x32 -> x24, local copies, waits for them, and re-layouts: 0.08 us -> 17 us
    another operation x12 -> x0, other arithmetic: 15.9 us -> none  [the longest x6 7.18 us: solve_factor(): lower = jnp.linalg.cholesky(gram)]
    div x3 -> x0, other arithmetic: 3.95 us -> none  [the longest x1 2.36 us: on_device(): q_up_next = q_up_rows / replicas]
  transfers between devices with their start and end apart: 3 -> 0, of which waited for: 3 -> 0; matrix products, arithmetic and copies ran while one was open for 1% -> 0% of each run, Pallas kernels for 0% -> 0%
where the time goes in v1:
time: 128 us
  Pallas kernels  110 us (86%)
  local copies, waits for them, and re-layouts  17 us (13%)
    pallas_call x1, Pallas kernels, on_device(): pl.pallas_call(functools.partial(exchange_kernel, n_dp, n_mp), out_shape=...  95.6 us
    unnamed x24, local copies, waits for them, and re-layouts  17 us
    pallas_call x1, Pallas kernels, on_device(): pl.pallas_call(momentum_kernel, grid=(large // step,), out_shape=(jax.Sha...  14.4 us

profile of v1, /device:TPU:0, one launch (start us, length us, event | category | flops | bytes accessed | tf_op | source)
XLA Modules:
  0.0 127.6 jit_solution(9522853120995431076)
XLA Ops:
  0.6 0.0 copy-start.1
  0.6 1.7 %copy-done.1 = bf16[128,9216]{1,0:T(8,128)(2,1)S(1)} copy-done((bf16[128,9216]{1,0:T(8,128)(2,1)S(1)}, bf16[128,9216]{1,0:T(8,128)(2,1)}, u32[]{:S(2)}) %copy-start.1) | copy-done | bytes 2359320
  2.3 0.0 copy-start.2
  2.3 1.7 %copy-done.2 = bf16[128,9216]{1,0:T(8,128)(2,1)S(1)} copy-done((bf16[128,9216]{1,0:T(8,128)(2,1)S(1)}, bf16[128,9216]{1,0:T(8,128)(2,1)}, u32[]{:S(2)}) %copy-start.2) | copy-done | bytes 2359320
  4.0 0.0 copy-start.3
  4.0 1.3 copy-done.3
  5.2 0.0 copy-start.4
  5.2 1.1 copy-done.4
  6.3 0.0 copy-start.5
  6.3 1.1 copy-done.5
  7.4 0.0 copy-start.6
  7.4 1.0 copy-done.6
  8.3 0.0 copy-start.7
  8.3 1.0 copy-done.7
  9.3 0.0 copy-start.8
  9.3 0.9 copy-done.8
  10.2 0.0 copy-start.9
  10.2 0.9 copy-done.9
  11.1 0.0 copy-start.10
  11.1 0.9 copy-done.10
  12.0 95.6 %shard_map.147 = (f32[32,9216]{1,0:T(8,128)S(1)}, f32[32,1152]{1,0:T(8,128)S(1)}, bf16[96,576]{1,0:T(8,128)(2,1)S(1)}, bf16[96,9216]{1,0:T(8,128)(2,1)S(1)}, bf1...) custom-call(bf16[128,1152]{1,0:T(8,128)(2,1)S(1)} %copy-done.6, bf16[128,9216]{1,0:T(8,128)(2,1)S(1)} %copy-done.1, ...), custom_call_target="tpu_custom_call" | custom-call | tf_op jit(solution)/shard_map/pallas_call | solution.py:550
  107.5 0.0 copy-start
  107.6 4.0 %copy-done = bf16[576,9216]{1,0:T(8,128)(2,1)S(1)} copy-done((bf16[576,9216]{1,0:T(8,128)(2,1)S(1)}, bf16[576,9216]{1,0:T(8,128)(2,1)}, u32[]{:S(2)}) %copy-start) | copy-done | bytes 10616856
  111.6 14.4 %shard_map.148 = (bf16[576,9216]{1,0:T(8,128)(2,1)}, bf16[576,9216]{1,0:T(8,128)(2,1)}) custom-call(bf16[576,9216]{1,0:T(8,128)(2,1)S(1)} %copy-done, bf16[576,9216]{1,0:T(8,128)(2,1)} %bitcast.26, bf16[96,576]{1,0:T(8,128)(2,1)S(1)} %get-tuple-element.14.a_up, bf16[96,9216]{1,0:T(8,128)(2,1)S(1)} %get-tuple-element.15.b_up, ...), custom_call_target="tpu_custom_call" | custom-call | tf_op jit(solution)/shard_map/pallas_call | solution.py:600
  126.0 1.0 copy.18
  127.0 0.7 copy.19
Async XLA Ops:
  0.6 1.7 %copy-start.1 = (bf16[128,9216]{1,0:T(8,128)(2,1)S(1)}, bf16[128,9216]{1,0:T(8,128)(2,1)}, u32[]{:S(2)}) copy-start(bf16[128,9216]{1,0:T(8,128)(2,1)} %up_grad.1) | copy-start | bytes 7077892
  2.3 1.7 %copy-start.2 = (bf16[128,9216]{1,0:T(8,128)(2,1)S(1)}, bf16[128,9216]{1,0:T(8,128)(2,1)}, u32[]{:S(2)}) copy-start(bf16[128,9216]{1,0:T(8,128)(2,1)} %hidden.1) | copy-start | bytes 7077892
  4.0 1.3 copy-start.3
  5.2 1.1 copy-start.4
  6.3 1.1 copy-start.5
  7.4 1.0 copy-start.6
  8.3 1.0 copy-start.7
  9.3 0.9 copy-start.8
  10.2 0.9 copy-start.9
  11.1 0.9 copy-start.10
  107.5 4.0 %copy-start = (bf16[576,9216]{1,0:T(8,128)(2,1)S(1)}, bf16[576,9216]{1,0:T(8,128)(2,1)}, u32[]{:S(2)}) copy-start(bf16[576,9216]{1,0:T(8,128)(2,1)} %m_up.1) | copy-start | bytes 31850500

commit v2 on v1

--- a/solution.py
+++ b/solution.py
@@ -126,48 +126,43 @@
 def exchange_kernel(
     n_dp,
     n_mp,
-    layer_in,
-    up_grad,
-    hidden,
-    out_grad,
-    eul,
-    eur,
-    edl,
-    edr,
-    q_up,
-    q_down,
-    q_up_out,
-    q_down_out,
-    a_up,
-    b_up,
-    a_down,
-    b_down,
-    pay_a,
-    got_a,
-    pay_b,
-    got_b,
-    work_p,
-    core_p,
-    right_p,
-    left_p,
-    full_p,
-    work_q,
-    core_q,
-    right_q,
-    left_q,
-    full_q,
-    p_block,
-    q_block,
-    mp_send,
-    mp_recv,
-    core_sem,
-    line_send,
-    line_recv,
-    pair_send,
-    pair_recv,
-    block_send,
-    block_recv,
+    *refs,
 ):
+    operands, outputs, held = refs[:12], refs[12:18], refs[18:28]
+    full_q, m_up, m_down, b_down, a_up, q_block = outputs
+    (
+        pay_a,
+        got_a,
+        pay_b,
+        got_b,
+        work_p,
+        pair_p,
+        right_p,
+        left_p,
+        full_p,
+        work_q,
+        pair_q,
+        right_q,
+        left_q,
+        p_block,
+        load_sem,
+        mp_send,
+        mp_recv,
+        swap_send,
+        swap_recv,
+        line_send,
+        line_recv,
+        mate_send,
+        mate_recv,
+        block_send,
+        block_recv,
+    ) = refs[28:]
+    layer_in, up_grad, hidden, out_grad, eul, eur, edl, edr, q_up, q_down = held
+    landing = (*held, m_up, m_down)
+    loads = [pltpu.make_async_copy(operands[i], landing[i], load_sem.at[i]) for i in range(12)]
+    first_loads, second_loads, last_loads = (8, 1, 5, 9, 3, 7), (0, 4, 2, 6), (10, 11)
+    for i in first_loads + second_loads + last_loads:
+        loads[i].start()
     dp = lax.axis_index("dp")
     mp = lax.axis_index("mp")
     chips = n_dp // 2
@@ -178,10 +173,10 @@
     small = layer_in.shape[1]
     small_pad = whole_tiles(small)
     large = hidden.shape[1]
-    block = a_up.shape[1]
+    block = m_up.shape[0]
     per_shard = small // block
     owner = dp // per_shard
-    half = core_p.shape[1]
+    half = pair_p.shape[1]
     piece = half // (chips // 4)
     mate = (dp + 1 - 2 * core, mp)
     right = (dp + 2, mp)
@@ -233,25 +228,33 @@
             total = total + got[lax.rem(mp + n_mp - i, n_mp)]
         return total
 
-    def all_reduce(work, pair, to_right, to_left, full, which):
+    def all_reduce(work, pair, to_right, to_left, full, which, meanwhile):
         def at_piece(ref, s, base):
             rows = pl.ds(pl.multiple_of(8 * lax.rem(s, 4), 8), 8)
             return ref.at[rows, pl.ds(pl.multiple_of(base + (s // 4) * piece, LANES), piece)]
 
         mine = core * half
         theirs = (1 - core) * half
-        swap = remote(
-            work.at[:, pl.ds(pl.multiple_of(theirs, LANES), half)],
-            pair,
-            core_sem.at[which, 0],
-            core_sem.at[which, 1],
-            mate,
-        )
-        swap.start()
-        swap.wait()
-
-        own = pl.ds(pl.multiple_of(mine, LANES), half)
-        pair[...] += work[:, own]
+
+        def swap(s):
+            return remote(
+                at_piece(work, s, theirs),
+                at_piece(pair, s, 0),
+                swap_send.at[which, s],
+                swap_recv.at[which, s],
+                mate,
+            )
+
+        def start_swap(t, carry):
+            swap(jnp.where(lax.rem(t, 2) == 0, chips - 1 - t // 2, t // 2)).start()
+            return carry
+
+        lax.fori_loop(0, chips, start_swap, 0)
+
+        def add_mate(s):
+            swap(s).wait_recv()
+            at = at_piece(pair, s, 0)
+            at[...] = at[...] + at_piece(work, s, mine)[...]
 
         def hop(buf, way, s, to):
             return remote(
@@ -280,6 +283,8 @@
 
             @pl.when((k >= chip) & (chip < chips - 1))
             def _():
+                add_mate(s)
+
                 @pl.when(chip > 0)
                 def _():
                     hop(to_right, 0, s, right).wait_recv()
@@ -294,6 +299,8 @@
 
             @pl.when((z >= 0) & (chip > 0))
             def _():
+                add_mate(z)
+
                 @pl.when(chip < chips - 1)
                 def _():
                     hop(to_left, 1, z, left).wait_recv()
@@ -306,7 +313,10 @@
 
             return carry
 
-        lax.fori_loop(0, chips - 1, reduce_step, 0)
+        reduce_step(0, 0)
+        meanwhile()
+        lax.fori_loop(1, chips - 1, reduce_step, 0)
+        add_mate(chip)
 
         mine_here = at_piece(pair, chip, 0)
 
@@ -335,8 +345,8 @@
             return remote(
                 at_piece(full, s, mine),
                 at_piece(full, s, mine),
-                pair_send.at[which, s],
-                pair_recv.at[which, s],
+                mate_send.at[which, s],
+                mate_recv.at[which, s],
                 mate,
             )
 
@@ -344,8 +354,8 @@
             return remote(
                 at_piece(full, s, theirs),
                 at_piece(full, s, theirs),
-                pair_send.at[which, s],
-                pair_recv.at[which, s],
+                mate_send.at[which, s],
+                mate_recv.at[which, s],
                 mate,
             )
 
@@ -388,6 +398,7 @@
 
         def drain(s, carry):
             from_mate(s).wait_recv()
+            swap(s).wait_send()
             to_mate(s).wait_send()
 
             @pl.when(chip < s)
@@ -439,6 +450,8 @@
         rolled = pltpu.roll(full[:, :small_pad], shift, 1)
         buf[...] = rolled[:, : buf.shape[1]]
 
+    for i in first_loads:
+        loads[i].wait()
     pay_a[...] = jnp.zeros_like(pay_a)
     pay_a[0, :, : tokens + rank] = fold3(project(q_up, 0, up_grad, eur, False))
     pay_a[1, :, : tokens + rank] = fold3(project(q_down, 0, out_grad, edr, False))
@@ -448,9 +461,11 @@
         for a, b in ((small // LANES * LANES, small_pad), (small_pad + large, work.shape[1])):
             if b > a:
                 work[:, a:b] = jnp.zeros((rank, b - a), F32)
+    for i in second_loads:
+        loads[i].wait()
     expand(total[0, :, : tokens + rank], layer_in, eul, work_p, 0)
     expand(total[1, :, : tokens + rank], hidden, edl, work_p, small_pad)
-    all_reduce(work_p, core_p, right_p, left_p, full_p, 0)
+    all_reduce(work_p, pair_p, right_p, left_p, full_p, 0, lambda: None)
 
     @pl.when(mp == owner)
     def _():
@@ -467,48 +482,105 @@
     t_down = dot_small(inv_down, total[1])[:, : tokens + rank]
     expand(t_down, out_grad, edr, work_q, 0)
     expand(t_up, up_grad, eur, work_q, small_pad)
-    all_reduce(work_q, core_q, right_q, left_q, full_q, 1)
+
+    def orthonormal():
+        step = chunk_of(large)
+
+        def body(i, carry):
+            at = pl.multiple_of(i * step, LANES)
+            orth = dot_small(inv_down, full_p[:, pl.ds(small_pad + at, step)])
+            b_down[:, pl.ds(at, step)] = split_right(orth)
+            return carry
+
+        lax.fori_loop(0, large // step, body, 0)
+
+    all_reduce(work_q, pair_q, right_q, left_q, full_q, 1, orthonormal)
 
     @pl.when(mp == owner)
     def _():
         pick_block(full_q, q_block)
         send_block(q_block, 1)
 
-    q_down_out[...] = full_q[:, :small]
-
-    def split_left(x):
-        hi = x.astype(BF16)
-        return jnp.concatenate([hi, hi, (x - hi.astype(F32)).astype(BF16)], axis=0)
-
-    def split_right(x):
-        hi = x.astype(BF16)
-        return jnp.concatenate([hi, (x - hi.astype(F32)).astype(BF16), hi], axis=0)
-
-    step = chunk_of(large)
-
-    def finish(i, carry):
+    wait_block(p_block, 0)
+    a_up[...] = dot_small(inv_up, p_block[...])
+    for i in last_loads:
+        loads[i].wait()
+    wait_block(q_block, 1)
+
+
+def split_right(x):
+    hi = x.astype(BF16)
+    return jnp.concatenate([hi, (x - hi.astype(F32)).astype(BF16), hi], axis=0)
+
+
+def split_left(x):
+    hi = x.astype(BF16).astype(F32)
+    return jnp.concatenate([hi, hi, x - hi], axis=0).T.astype(BF16)
+
+
+def momentum_kernel(
+    small,
+    full_q,
+    m_up,
+    m_down,
+    b_down,
+    a_up,
+    a_down,
+    q_up_out,
+    q_down_out,
+    out_up,
+    out_down,
+    buf_up,
+    buf_down,
+    left_up,
+    left_down,
+    q_small,
+    sem_up,
+    sem_down,
+    sem_q,
+):
+    block, large = m_up.shape
+    step = buf_up.shape[2]
+    start = whole_tiles(small)
+    q_small[...] = full_q[:, :small]
+    q_copies = (
+        pltpu.make_async_copy(full_q.at[:, pl.ds(start, large)], q_up_out, sem_q.at[0]),
+        pltpu.make_async_copy(q_small, q_down_out, sem_q.at[1]),
+    )
+    left_up[...] = split_left(a_up[...])[:block]
+    left_down[...] = split_left(a_down[...])[:block]
+
+    def copy(buf, out, sem, i):
+        columns = pl.ds(pl.multiple_of(i * step, LANES), step)
+        return pltpu.make_async_copy(buf.at[i % 2], out.at[:, columns], sem.at[i % 2])
+
+    def body(i, carry):
         at = pl.multiple_of(i * step, LANES)
-        orth = dot_small(inv_down, full_p[:, pl.ds(small_pad + at, step)])
-        b_down[:, pl.ds(at, step)] = split_right(orth)
-        q = full_q[:, pl.ds(small_pad + at, step)]
-        q_up_out[:, pl.ds(at, step)] = q
-        b_up[:, pl.ds(at, step)] = split_right(q)
+        columns = pl.ds(at, step)
+        q = split_right(full_q[:, pl.ds(start + at, step)])
+        for m, a, b, buf, out, sem in (
+            (m_up, left_up, q, buf_up, out_up, sem_up),
+            (m_down, left_down, b_down[:, columns], buf_down, out_down, sem_down),
+        ):
+
+            @pl.when(i >= 2)
+            def _():
+                copy(buf, out, sem, i - 2).wait()
+
+            delta = dot_nn(a[...], b)
+            buf[i % 2] = (0.9 * m[:, columns].astype(F32) + delta).astype(BF16)
+            copy(buf, out, sem, i).start()
         return carry
 
-    lax.fori_loop(0, large // step, finish, 0)
-
-    wait_block(p_block, 0)
-    a_up[...] = split_left(dot_small(inv_up, p_block[...]))[:, :block]
-    wait_block(q_block, 1)
-    a_down[...] = split_left(q_block[...])[:, :block]
-
-
-def momentum_kernel(m_up, m_down, a_up, b_up, a_down, b_down, out_up, out_down):
-    for m, a, b, out in ((m_up, a_up, b_up, out_up), (m_down, a_down, b_down, out_down)):
-        delta = lax.dot_general(
-            a[...], b[...], (((0,), (0,)), ((), ())), preferred_element_type=F32
-        )
-        out[...] = (0.9 * m[...].astype(F32) + delta).astype(BF16)
+    count = large // step
+    lax.fori_loop(0, count, body, 0)
+    for c in q_copies:
+        c.start()
+    for i in range(max(count - 2, 0), count):
+        copy(buf_up, out_up, sem_up, i).wait()
+        copy(buf_down, out_down, sem_down, i).wait()
+    for c in q_copies:
+        c.wait()
 
 
 def on_device(
@@ -537,51 +609,9 @@
     piece = -(-((whole_tiles(small) + large) // LANES) // pieces) * LANES
     half = piece * pieces // 2
     vmem = pl.BlockSpec(memory_space=pltpu.VMEM)
+    hbm = pl.BlockSpec(memory_space=pltpu.HBM)
     dma = pltpu.SemaphoreType.DMA
-    reduce_buffers = [
-        pltpu.VMEM((rank, 2 * half), F32),
-        pltpu.VMEM((rank, half), F32),
-        pltpu.VMEM((rank, half), F32),
-        pltpu.VMEM((rank, half), F32),
-        pltpu.VMEM((rank, 2 * half), F32),
-    ]
-    pay = pltpu.VMEM((2, rank, tokens + 4 * rank), F32)
-    got = pltpu.VMEM((n_mp, 2, rank, tokens + 4 * rank), F32)
-    q_up_t, q_down_t, a_up, b_up, a_down, b_down = pl.pallas_call(
-        functools.partial(exchange_kernel, n_dp, n_mp),
-        out_shape=(
-            jax.ShapeDtypeStruct((rank, large), F32),
-            jax.ShapeDtypeStruct((rank, small), F32),
-            jax.ShapeDtypeStruct((3 * rank, block), BF16),
-            jax.ShapeDtypeStruct((3 * rank, large), BF16),
-            jax.ShapeDtypeStruct((3 * rank, block), BF16),
-            jax.ShapeDtypeStruct((3 * rank, large), BF16),
-        ),
-        in_specs=[vmem] * 10,
-        out_specs=[vmem] * 6,
-        scratch_shapes=[
-            pay,
-            got,
-            pay,
-            got,
-            *reduce_buffers,
-            *reduce_buffers,
-            pltpu.VMEM((rank, block_pad), F32),
-            pltpu.VMEM((rank, block_pad), F32),
-            dma((2, n_mp)),
-            dma((2, n_mp)),
-            dma((2, 2)),
-            dma((2, 4, chips)),
-            dma((2, 4, chips)),
-            dma((2, chips)),
-            dma((2, chips)),
-            dma((2, n_mp)),
-            dma((2,)),
-        ],
-        compiler_params=pltpu.CompilerParams(
-            collective_id=0, has_side_effects=True, vmem_limit_bytes=30 * 1024 * 1024
-        ),
-    )(
+    operands = (
         layer_in,
         up_grad,
         hidden,
@@ -592,22 +622,76 @@
         err_down_right[0].T,
         q_up.T,
         q_down.T,
+        momentum_up,
+        momentum_down.T,
     )
+    operands = tuple(pltpu.with_memory_space_constraint(x, pltpu.HBM) for x in operands)
+    whole = pltpu.VMEM((rank, 2 * half), F32)
+    part = pltpu.VMEM((rank, half), F32)
+    pay = pltpu.VMEM((2, rank, tokens + 4 * rank), F32)
+    got = pltpu.VMEM((n_mp, 2, rank, tokens + 4 * rank), F32)
+    full_q, m_up, m_down, b_down, a_up, a_down = pl.pallas_call(
+        functools.partial(exchange_kernel, n_dp, n_mp),
+        out_shape=(
+            jax.ShapeDtypeStruct((rank, 2 * half), F32),
+            jax.ShapeDtypeStruct((block, large), BF16),
+            jax.ShapeDtypeStruct((block, large), BF16),
+            jax.ShapeDtypeStruct((3 * rank, large), BF16),
+            jax.ShapeDtypeStruct((rank, block_pad), F32),
+            jax.ShapeDtypeStruct((rank, block_pad), F32),
+        ),
+        in_specs=[hbm] * 12,
+        out_specs=[vmem] * 6,
+        scratch_shapes=[
+            *[pltpu.VMEM(x.shape, x.dtype) for x in operands[:10]],
+            pay,
+            got,
+            pay,
+            got,
+            *[whole, part, part, part, whole],
+            *[whole, part, part, part],
+            pltpu.VMEM((rank, block_pad), F32),
+            dma((12,)),
+            dma((2, n_mp)),
+            dma((2, n_mp)),
+            dma((2, chips)),
+            dma((2, chips)),
+            dma((2, 4, chips)),
+            dma((2, 4, chips)),
+            dma((2, chips)),
+            dma((2, chips)),
+            dma((2, n_mp)),
+            dma((2,)),
+        ],
+        compiler_params=pltpu.CompilerParams(
+            collective_id=0, has_side_effects=True, vmem_limit_bytes=26 * 1024 * 1024
+        ),
+    )(*operands)
     step = chunk_of(large)
-    wide = pl.BlockSpec((block, step), lambda i: (0, i))
-    left = pl.BlockSpec((3 * rank, block), lambda i: (0, 0))
-    right = pl.BlockSpec((3 * rank, step), lambda i: (0, i))
-    new_up, new_down_t = pl.pallas_call(
-        momentum_kernel,
-        grid=(large // step,),
+    slots = pltpu.VMEM((2, block, step), BF16)
+    left = pltpu.VMEM((block, 3 * rank), BF16)
+    q_up_t, q_down_t, new_up, new_down_t = pl.pallas_call(
+        functools.partial(momentum_kernel, small),
         out_shape=(
+            jax.ShapeDtypeStruct((rank, large), F32),
+            jax.ShapeDtypeStruct((rank, small), F32),
             jax.ShapeDtypeStruct((block, large), BF16),
             jax.ShapeDtypeStruct((block, large), BF16),
         ),
-        in_specs=[wide, wide, left, right, left, right],
-        out_specs=[wide, wide],
-        compiler_params=pltpu.CompilerParams(vmem_limit_bytes=32 * 1024 * 1024),
-    )(momentum_up, momentum_down.T, a_up, b_up, a_down, b_down)
+        in_specs=[vmem] * 6,
+        out_specs=[hbm] * 4,
+        scratch_shapes=[
+            slots,
+            slots,
+            left,
+            left,
+            pltpu.VMEM((rank, small), F32),
+            dma((2,)),
+            dma((2,)),
+            dma((2,)),
+        ],
+        compiler_params=pltpu.CompilerParams(vmem_limit_bytes=16 * 1024 * 1024),
+    )(full_q, m_up, m_down, b_down, a_up, a_down)
     return (q_up_t.T, q_down_t.T, new_up, new_down_t.T)
 
 

time: 128 us -> 109 us (0.85)
  local copies, waits for them, and re-layouts: 17 us -> 0 us
  Pallas kernels: 110 us -> 108 us
    unnamed x24 -> x0, local copies, waits for them, and re-layouts: 17 us -> none
    pallas_call x1, Pallas kernels: 14.4 us -> 10.2 us  [on_device(): pl.pallas_call(functools.partial(momentum_kernel, small), out_shape=(jax....]
    pallas_call x1, Pallas kernels: 95.6 us -> 97.7 us  [on_device(): pl.pallas_call(functools.partial(exchange_kernel, n_dp, n_mp), out_shape=...]
where the time goes in v2:
time: 109 us; the launch traced here: 108 us
  Pallas kernels  108 us (99%)
    pallas_call x1, Pallas kernels, on_device(): pl.pallas_call(functools.partial(exchange_kernel, n_dp, n_mp), out_shape=...  97.7 us
    pallas_call x1, Pallas kernels, on_device(): pl.pallas_call(functools.partial(momentum_kernel, small), out_shape=(jax....  10.2 us

profile of v2, /device:TPU:0, one launch (start us, length us, event | category | flops | bytes accessed | tf_op | source)
XLA Modules:
  0.0 108.5 jit_solution(10979124433410380212)
XLA Ops:
  0.6 97.7 %shard_map.147 = (f32[32,10496]{1,0:T(8,128)S(1)}, bf16[576,9216]{1,0:T(8,128)(2,1)S(1)}, bf16[576,9216]{1,0:T(8,128)(2,1)S(1)}, bf16[96,9216]{1,0:T(8,128)(2,1)...) custom-call(bf16[128,1152]{1,0:T(8,128)(2,1)} %refs_0_.1, bf16[128,9216]{1,0:T(8,128)(2,1)} %refs_1_.1, ...), custom_call_target="tpu_custom_call" | custom-call | tf_op jit(solution)/shard_map/pallas_call | solution.py:633
  98.3 10.2 %shard_map.148 = (f32[32,9216]{1,0:T(8,128)}, f32[32,1152]{1,0:T(8,128)}, bf16[576,9216]{1,0:T(8,128)(2,1)}, bf16[576,9216]{1,0:T(8,128)(2,1)}) custom-call(f32[32,10496]{1,0:T(8,128)S(1)} %get-tuple-element.14.full_q, bf16[576,9216]{1,0:T(8,128)(2,1)S(1)} %get-tuple-element.15.m_up, bf16[576,9216]{1,0:T(8,128)(2,1)S(1)} %get-tuple-element.16.m_down, ...), custom_call_target="tpu_custom_call" | custom-call | tf_op jit(solution)/shard_map/pallas_call | solution.py:673

commit v3 on v2

--- a/solution.py
+++ b/solution.py
@@ -66,7 +66,7 @@
         return acc + dot_nt(x, jnp.concatenate(parts, axis=0))
 
     zero = jnp.zeros((3 * err_ref.shape[0], outs), F32)
-    return body(0, zero) if step == width else lax.fori_loop(0, width // step, body, zero)
+    return body(0, zero) if step == width else lax.fori_loop(0, width // step, body, zero, unroll=True)
 
 
 def expand(left, rows_ref, err_ref, out_ref, start):
@@ -83,7 +83,7 @@
     if step == width:
         body(0, 0)
     else:
-        lax.fori_loop(0, width // step, body, 0)
+        lax.fori_loop(0, width // step, body, 0, unroll=True)
 
 
 def gram_and_projections(acc, tokens):
@@ -112,10 +112,7 @@
     for k in range(rank - 1):
         pivot_row = a[k : k + 1, :]
         column = jnp.where(low, a[:, k : k + 1], a[:, 2 * rank + k : 2 * rank + k + 1])
-        pivot = jnp.where(
-            low[:1], pivot_row[:, k : k + 1], pivot_row[:, 2 * rank + k : 2 * rank + k + 1]
-        )
-        scaled = pivot_row / pivot
+        scaled = pivot_row / column[k : k + 1, :]
         a = a - jnp.where(row > k, column, 0.0) * scaled
     diag_up = jnp.sum(jnp.where(lane == row, a, 0.0), axis=1, keepdims=True)
     diag_down = jnp.sum(jnp.where(lane == row + 2 * rank, a, 0.0), axis=1, keepdims=True)
@@ -492,7 +489,7 @@
             b_down[:, pl.ds(at, step)] = split_right(orth)
             return carry
 
-        lax.fori_loop(0, large // step, body, 0)
+        lax.fori_loop(0, large // step, body, 0, unroll=True)
 
     all_reduce(work_q, pair_q, right_q, left_q, full_q, 1, orthonormal)
 

time: 109 us -> 107 us (0.982)
  Pallas kernels: 108 us -> 106 us
    pallas_call x1, Pallas kernels: 97.7 us -> 95.6 us  [on_device(): pl.pallas_call(functools.partial(exchange_kernel, n_dp, n_mp), out_shape=...]
where the time goes in v3:
time: 107 us; the launch traced here: 106 us
  Pallas kernels  106 us (99%)
    pallas_call x1, Pallas kernels, on_device(): pl.pallas_call(functools.partial(exchange_kernel, n_dp, n_mp), out_shape=...  95.6 us
    pallas_call x1, Pallas kernels, on_device(): pl.pallas_call(functools.partial(momentum_kernel, small), out_shape=(jax....  10.2 us

profile of v3, /device:TPU:0, one launch (start us, length us, event | category | flops | bytes accessed | tf_op | source)
XLA Modules:
  0.0 106.5 jit_solution(4232001207175507792)
XLA Ops:
  0.6 95.6 %shard_map.147 = (f32[32,10496]{1,0:T(8,128)S(1)}, bf16[576,9216]{1,0:T(8,128)(2,1)S(1)}, bf16[576,9216]{1,0:T(8,128)(2,1)S(1)}, bf16[96,9216]{1,0:T(8,128)(2,1)...) custom-call(bf16[128,1152]{1,0:T(8,128)(2,1)} %refs_0_.1, bf16[128,9216]{1,0:T(8,128)(2,1)} %refs_1_.1, ...), custom_call_target="tpu_custom_call" | custom-call | tf_op jit(solution)/shard_map/pallas_call | solution.py:630
  96.3 10.2 %shard_map.148 = (f32[32,9216]{1,0:T(8,128)}, f32[32,1152]{1,0:T(8,128)}, bf16[576,9216]{1,0:T(8,128)(2,1)}, bf16[576,9216]{1,0:T(8,128)(2,1)}) custom-call(f32[32,10496]{1,0:T(8,128)S(1)} %get-tuple-element.14.full_q, bf16[576,9216]{1,0:T(8,128)(2,1)S(1)} %get-tuple-element.15.m_up, bf16[576,9216]{1,0:T(8,128)(2,1)S(1)} %get-tuple-element.16.m_down, ...), custom_call_target="tpu_custom_call" | custom-call | tf_op jit(solution)/shard_map/pallas_call | solution.py:670
